TPU v7x, 128 devices: a whole 4x4x4 slice. The times are simulated.
128 devices in a mesh: ctx: 16 (over y, x), head: 8 (over z, core).
Axes of the slice: x: 4, y: 4, z: 4, core: 2. Of those that a mesh axis runs over, the one named last changes fastest.
Arguments:
- q_nope: bfloat16 [8, 128, 128], P(None, 'head'), may hold values from -6 to 6
- q_rope: bfloat16 [8, 128, 64], P(None, 'head'), may hold values from -10 to 10
- latent_cache: bfloat16 [8, 131072, 576], P(None, 'ctx'), may hold values from -8 to 8
- lengths: int32 [8], replicated, may hold values from 16384 to 131072, as said below
- w_key_absorb: bfloat16 [128, 128, 512], P('head'), may hold values from -0.5 to 0.5
- w_value_up: bfloat16 [128, 512, 128], P('head'), may hold values from -0.25 to 0.25
- w_output: bfloat16 [16384, 7168], P('head', 'ctx'), may hold values from -0.046875 to 0.046875
- w_gate: bfloat16 [16, 7168, 2048], P('ctx', None, 'head'), may hold values from -0.0625 to 0.0625
- w_up: bfloat16 [16, 7168, 2048], P('ctx', None, 'head'), may hold values from -0.0625 to 0.0625
- w_down: bfloat16 [16, 2048, 7168], P('ctx', 'head'), may hold values from -0.125 to 0.125
- expert_ids: int32 [8, 8], replicated, may hold values from 0 to 15, all different within a row
- gate_weights: float32 [8, 8], replicated, may hold values from 0.05 to 0.4
Outputs:
- attn_out: bfloat16 [8, 7168], P(None, 'ctx')
- expert_out: bfloat16 [8, 7168], P(None, ('ctx', 'head'))
Inputs may be any that keep to these rules, and one draw needn't show every extreme that they name: `lengths`: every row has at least 16384 valid positions and row 0 has all of them.
All inputs are finite; a program needn't handle non-finite values.
Results may differ from a plain program's by a relative error of at most 0.03.
Values may be sent and summed in bfloat16 or wider, within the bound.
A program may use at most 192 MiB of HBM per device.

v0:
```python
import jax
import jax.numpy as jnp
from jax import lax
from jax.sharding import PartitionSpec as P

NOPE = 128
ROPE = 64
LAT = 512


def merged(part, axis, combine):
    gathered = jax.tree.map(lambda a: lax.all_gather(a, axis), part)

    def take(source):
        return jax.tree.map(lambda a: lax.dynamic_index_in_dim(a, source, 0, False), gathered)

    return lax.fori_loop(
        1, lax.axis_size(axis), lambda source, state: combine(state, take(source)), take(0)
    )


def join_partials(first, second):
    peak = jnp.maximum(first[0], second[0])
    left = jnp.exp(first[0] - peak)
    right = jnp.exp(second[0] - peak)
    total = first[1] * left + second[1] * right
    summed = first[2] * left[..., None] + second[2] * right[..., None]
    return (peak, total, summed)


def attend(query, cache, row_lengths, offset):
    scale = (NOPE + ROPE) ** (-0.5)
    span = cache.shape[1]
    positions = offset + jnp.arange(span, dtype=jnp.int32)
    score = jnp.einsum("bhc,btc->bht", query, cache, preferred_element_type=jnp.float32) * scale
    valid = positions[None, None, :] < row_lengths[:, None, None]
    peak = jnp.max(jnp.where(valid, score, -1e30), axis=-1)
    weight = jnp.where(valid, jnp.exp(score - peak[..., None]), 0.0)
    total = jnp.sum(weight, axis=-1)
    summed = jnp.einsum(
        "bht,btl->bhl",
        weight.astype(jnp.bfloat16),
        cache[:, :, :LAT],
        preferred_element_type=jnp.float32,
    )
    return (peak, total, summed)


def combine_slices(peak, total, summed):
    peak, total, summed = merged((peak, total, summed), "ctx", join_partials)
    return (summed / total[..., None]).astype(jnp.bfloat16)


def body(
    q_nope,
    q_rope,
    latent_cache,
    lengths,
    w_key_absorb,
    w_value_up,
    w_output,
    w_gate,
    w_up,
    w_down,
    expert_ids,
    gate_weights,
):
    rows = q_nope.shape[0]
    q_latent = jnp.einsum(
        "bhn,hnl->bhl", q_nope, w_key_absorb, preferred_element_type=jnp.float32
    ).astype(jnp.bfloat16)
    query = jnp.concatenate([q_latent, q_rope], axis=-1)
    offset = lax.axis_index("ctx") * latent_cache.shape[1]
    peak, total, summed = attend(query, latent_cache, lengths, offset)
    o_latent = combine_slices(peak, total, summed)
    head_out = jnp.einsum(
        "bhl,hln->bhn", o_latent, w_value_up, preferred_element_type=jnp.float32
    ).astype(jnp.bfloat16)
    head_out = head_out.reshape(rows, -1)
    partial_proj = jnp.dot(head_out, w_output, preferred_element_type=jnp.float32)
    attn_out = lax.psum(partial_proj, "head").astype(jnp.bfloat16)
    features = lax.all_gather(attn_out, "ctx", axis=1, tiled=True)
    wide = features.astype(jnp.float32)
    normed = (wide / jnp.sqrt(jnp.mean(wide * wide, axis=-1, keepdims=True) + 1e-06)).astype(
        jnp.bfloat16
    )
    mine = lax.axis_index("ctx")
    select = jnp.sum(gate_weights * (expert_ids == mine).astype(jnp.float32), axis=1)
    gate = jnp.dot(normed, w_gate[0], preferred_element_type=jnp.float32)
    upper = jnp.dot(normed, w_up[0], preferred_element_type=jnp.float32)
    hidden = (jax.nn.silu(gate) * upper).astype(jnp.bfloat16)
    result = jnp.dot(hidden, w_down[0], preferred_element_type=jnp.float32) * select[:, None]
    expert_out = lax.psum_scatter(result, ("ctx", "head"), scatter_dimension=1, tiled=True).astype(
        jnp.bfloat16
    )
    return (attn_out, expert_out)


def solution(mesh):
    return jax.shard_map(
        body,
        mesh=mesh,
        in_specs=(
            P(None, "head", None),
            P(None, "head", None),
            P(None, "ctx", None),
            P(),
            P("head", None, None),
            P("head", None, None),
            P("head", "ctx"),
            P("ctx", None, "head"),
            P("ctx", None, "head"),
            P("ctx", "head", None),
            P(),
            P(),
        ),
        out_specs=(P(None, "ctx"), P(None, ("ctx", "head"))),
        check_vma=False,
    )
```

profile of v0, /device:TPU:1, one launch (start us, length us, event | category | flops | bytes accessed | tf_op | source)
XLA Modules:
  0.0 271.2 jit_solution(7608450080655570873)
XLA Ops:
  7.2 0.0 copy-start
  7.2 0.0 all-gather.6.cloned.1.call-start
  7.2 0.9 copy.20
  8.2 0.8 broadcast_compare_fusion
  8.9 0.0 copy-done
  8.9 1.1 fusion.16
  10.1 28.7 %select_reduce_fusion = (f32[8,16]{1,0:T(8,128)S(1)}, f32[8,16,8192]{2,1,0:T(8,128)}) fusion(pred[8,8192]{1,0:T(8,128)(4,1)S(1)} %broadcast_compare_fusion, bf16[8,8192,576]{1,2,0:T(8,128)(2,1)} %param.16, bf16[8,16,576]{2,0,1:T(8,128)(2,1)S(1)} %pad_maximum_fusion), kind=kOutput, calls=%fused_computation.13 | convolution fusion | flops 1211105152 | bytes 79905280 | tf_op jit(solution)/shard_map/bhc,btc->bht/dot_general | solution.py:35
  38.8 27.1 %fusion.3 = f32[8,16,512]{2,1,0:T(8,128)} fusion(bf16[8,8192,576]{1,2,0:T(8,128)(2,1)} %param.16, f32[8,16,8192]{2,1,0:T(8,128)} %get-tuple-element.200, f32[8,16]{1,0:T(8,128)S(1)} %get-tuple-element.199, pred[8,8192]{1,0:T(8,128)(4,1)S(1)} %broadcast_compare_fusion), kind=kOutput, calls=%fused_computation.8 | convolution fusion | flops 1076887552 | bytes 71631360 | tf_op jit(solution)/shard_map/bht,btl->bhl/dot_general | solution.py:40
  65.9 0.0 copy-start.2
  65.9 0.0 copy-start.3
  65.9 0.0 all-gather.6.cloned.1.call-update
  66.0 19.7 %all-gather = f32[128,16]{1,0:T(8,128)S(1)} all-gather(f32[8,16]{1,0:T(8,128)S(1)} %get-tuple-element.199), channel_id=2, replica_groups=mesh['ctx'=16,'head'=8] {'ctx'}, dimensions={0}, use_global_device_ids=true | all-gather | bytes 8704 | tf_op jit(solution)/shard_map/all_gather | solution.py:12
  85.7 3.3 %fusion.11 = f32[8,16]{1,0:T(8,128)S(1)} fusion(f32[8,16,8192]{2,1,0:T(8,128)} %get-tuple-element.200, f32[8,16]{1,0:T(8,128)S(1)} %get-tuple-element.199, pred[8,8192]{1,0:T(8,128)(4,1)S(1)} %broadcast_compare_fusion), kind=kLoop, calls=%fused_computation.20 | loop fusion | flops 3145600 | bytes 4260864 | tf_op jit(solution)/shard_map/reduce_sum | solution.py:39
  89.0 18.5 %all-gather.1 = f32[128,16]{1,0:T(8,128)S(1)} all-gather(f32[8,16]{1,0:T(8,128)S(1)} %fusion.11), channel_id=3, replica_groups=mesh['ctx'=16,'head'=8] {'ctx'}, dimensions={0}, use_global_device_ids=true | all-gather | bytes 8704 | tf_op jit(solution)/shard_map/all_gather | solution.py:12
  107.5 0.0 copy-done.2
  107.5 0.0 copy-done.3
  107.5 0.1 select_reduce_fusion.1
  107.6 13.5 %all-gather.6.cloned.1.call-done = f32[128,16,512]{2,1,0:T(8,128)} async-done(((f32[8,16,512]{2,1,0:T(8,128)}), f32[128,16,512]{2,1,0:T(8,128)}) %all-gather.6.cloned.1.call-update) | async-done | bytes 4194320 | tf_op jit(solution)/shard_map/all_gather | solution.py:12
  121.2 1.0 slice.12
  122.1 16.8 %while.19 = (s32[]{:T(128)}, f32[8,16]{1,0:T(8,128)S(1)}, f32[8,16]{1,0:T(8,128)S(1)}, f32[8,16,512]{2,1,0:T(8,128)S(1)}, f32[16,8,16]{2,1,0:T(8,128)S(1)}, /*in...) while((s32[]{:T(128)}, f32[8,16]{1,0:T(8,128)S(1)}, ...), condition=%wide.region_3.4_spmd, body=%wide.region_2.3_spmd.sunk | while | flops 197381 | bytes 791703 | solution.py:17
  122.2 1.1 fusion.47
  123.3 1.1 fusion.47
  124.4 1.1 fusion.47
  125.5 1.1 fusion.47
  126.7 1.1 fusion.47
  127.8 1.1 fusion.47
  128.9 1.1 fusion.47
  130.0 1.1 fusion.47
  131.1 1.1 fusion.47
  132.3 1.1 fusion.47
  133.4 1.1 fusion.47
  134.5 1.1 fusion.47
  135.6 1.1 fusion.47
  136.7 1.1 fusion.47
  137.9 1.1 fusion.47
  139.0 0.1 divide_convert_fusion
  139.1 3.0 %fusion.26 = f32[8,448]{1,0:T(8,128)S(1)} fusion(bf16[2048,448]{0,1:T(8,128)(2,1)} %param.20, bf16[16,512,128]{2,1,0:T(8,128)(2,1)} %param.19, bf16[8,16,512]{2,1,0:T(8,128)(2,1)S(1)} %divide_convert_fusion), kind=kOutput, calls=%fused_computation.30 | convolution fusion | flops 31473664 | bytes 4077568 | tf_op jit(solution)/shard_map/dot_general | solution.py:80
  142.1 22.9 %psum.7 = bf16[8,448]{1,0:T(8,128)(2,1)S(1)} all-reduce(f32[8,448]{1,0:T(8,128)S(1)} %fusion.26), channel_id=1, replica_groups=mesh['ctx'=16,'head'=8] {'head'}, use_global_device_ids=true, to_apply=%region_4.5 | all-reduce | flops 3584 | bytes 21504 | tf_op jit(solution)/shard_map/psum | solution.py:81
  165.0 0.0 copy-start.1
  165.0 18.3 %all-gather.3 = bf16[16,448,8]{1,2,0:T(8,128)(2,1)S(1)} all-gather(bf16[1,448,8]{1,2,0:T(8,128)(2,1)S(1)} %bitcast.59), channel_id=1, replica_groups=mesh['ctx'=16,'head'=8] {'ctx'}, dimensions={0}, use_global_device_ids=true | all-gather | bytes 121856 | tf_op jit(solution)/shard_map/all_gather | solution.py:82
  183.4 0.1 reshape.65
  183.5 0.2 multiply_reduce_fusion
  183.7 2.7 fusion.8
  186.3 5.3 %convolution_multiply_fusion.1 = f32[8,7168]{1,0:T(8,128)S(1)} fusion(bf16[1,256,7168]{2,1,0:T(8,128)(2,1)} %param.23, bf16[1,7168,256]{2,1,0:T(8,128)(2,1)} %param.22, f32[8]{0:T(128)S(1)} %select_reduce_fusion.1, f32[8,256]{1,0:T(8,128)S(1)} %fusion.8, f32[7168,8]{0,1:T(8,128)S(1)} %reshape.65, f32[8]{0:T(128)S(1)} %add_sqrt_fusion), kind=kOutput, calls=%fused_computation.11 | convolution fusion | flops 58904576 | bytes 7807040 | tf_op jit(solution)/shard_map/dot_general | solution.py:92
  191.6 0.0 copy-done.1
  191.6 72.1 %all-reduce.2 = bf16[8,7168]{1,0:T(8,128)(2,1)S(1)} all-reduce(f32[8,7168]{1,0:T(8,128)S(1)} %convolution_multiply_fusion.1), channel_id=5, replica_groups=mesh['ctx'=16,'head'=8] {'ctx','head'}, use_global_device_ids=true, to_apply=%region_7.8.clone | all-reduce | flops 57344 | bytes 344064
  263.7 0.7 dynamic-slice_convert_fusion
  (21 shorter events, 0.3 us)
Async XLA Ops:
  7.2 1.8 copy-start
  7.2 114.0 %all-gather.6.cloned.1.call-start = ((), (), s32[]{:S(2)}) async-start(), calls=%async_computation | async-start | bytes 4456448 | tf_op jit(solution)/shard_map/all_gather | solution.py:12
  65.9 41.6 %copy-start.2 = (f32[8,8]{1,0:T(8,128)S(1)}, f32[8,8]{1,0:T(8,128)}, u32[]{:S(2)}) copy-start(f32[8,8]{1,0:T(8,128)} %param.25) | copy-start | bytes 772
  65.9 41.6 %copy-start.3 = (s32[8,8]{1,0:T(8,128)S(1)}, s32[8,8]{1,0:T(8,128)}, u32[]{:S(2)}) copy-start(s32[8,8]{1,0:T(8,128)} %param.24) | copy-start | bytes 772
  165.0 26.6 %copy-start.1 = (bf16[8,448]{1,0:T(8,128)(2,1)}, bf16[8,448]{1,0:T(8,128)(2,1)S(1)}, u32[]{:S(2)}) copy-start(bf16[8,448]{1,0:T(8,128)(2,1)S(1)} %psum.7) | copy-start | bytes 21508
Sparse Core Ops, SparseCore 0:
  66.1 55.0 all-gather.5
where the time goes:
time: 272 us; the launch traced here: 271 us
  blocking collectives  152 us (56%)
  matrix products  67.9 us (25%)
  other arithmetic  20.8 us (8%)
  between operations  14.1 us (5%)
  waiting for transfers between devices  13.5 us (5%)
  local copies, waits for them, and re-layouts  2.74 us (1%)
    unnamed x1, blocking collectives  72.1 us
    all_gather x2, blocking collectives, merged(): gathered = jax.tree.map(lambda a: lax.all_gather(a, axis), part)  38.2 us
    dot_general x1, matrix products, attend(): jnp.einsum('bhc,btc->bht', query, cache, preferred_element_type=jnp.float32)  28.7 us
    dot_general x1, matrix products, attend(): jnp.einsum('bht,btl->bhl', weight.astype(jnp.bfloat16), cache[:, :, :LAT]...  27.1 us
    psum x1, blocking collectives, body(): attn_out = lax.psum(partial_proj, 'head').astype(jnp.bfloat16)  22.9 us
    all_gather x1, blocking collectives, body(): features = lax.all_gather(attn_out, 'ctx', axis=1, tiled=True)  18.3 us
    add x15, other arithmetic, join_partials(): summed = first[2] * left[..., None] + second[2] * right[..., None]  16.1 us
    all_gather x1, waiting for transfers between devices, merged(): gathered = jax.tree.map(lambda a: lax.all_gather(a, axis), part)  13.5 us
  transfers between devices with their start and end apart: 1, of which 1 were waited for; matrix products, arithmetic and copies ran while one was open for 1% of the time, Pallas kernels for 0%

commit v1 on v0

--- a/solution.py
+++ b/solution.py
@@ -78,7 +78,7 @@
     ).astype(jnp.bfloat16)
     head_out = head_out.reshape(rows, -1)
     partial_proj = jnp.dot(head_out, w_output, preferred_element_type=jnp.float32)
-    attn_out = lax.psum(partial_proj, "head").astype(jnp.bfloat16)
+    attn_out = jnp.sum(lax.all_gather(partial_proj, "head"), axis=0).astype(jnp.bfloat16)
     features = lax.all_gather(attn_out, "ctx", axis=1, tiled=True)
     wide = features.astype(jnp.float32)
     normed = (wide / jnp.sqrt(jnp.mean(wide * wide, axis=-1, keepdims=True) + 1e-06)).astype(

time: 272 us -> 260 us (0.956)
  blocking collectives: 152 us -> 139 us
    psum x1 -> x0, blocking collectives: 22.9 us -> none  [body(): attn_out = lax.psum(partial_proj, 'head').astype(jnp.bfloat16)]
    all_gather x0 -> x1, blocking collectives: none -> 13.9 us  [body(): lax.all_gather(partial_proj, 'head')]
    unnamed x1, blocking collectives: 72.1 us -> 68.6 us
where the time goes in v1:
time: 260 us; the launch traced here: 259 us
  blocking collectives  139 us (53%)
  matrix products  67.9 us (26%)
  other arithmetic  20.8 us (8%)
  between operations  14.1 us (5%)
  waiting for transfers between devices  13.5 us (5%)
  local copies, waits for them, and re-layouts  2.74 us (1%)
    unnamed x1, blocking collectives  68.6 us
    all_gather x2, blocking collectives, merged(): gathered = jax.tree.map(lambda a: lax.all_gather(a, axis), part)  38.2 us
    dot_general x1, matrix products, attend(): jnp.einsum('bhc,btc->bht', query, cache, preferred_element_type=jnp.float32)  28.7 us
    dot_general x1, matrix products, attend(): jnp.einsum('bht,btl->bhl', weight.astype(jnp.bfloat16), cache[:, :, :LAT]...  27.1 us
    all_gather x1, blocking collectives, body(): features = lax.all_gather(attn_out, 'ctx', axis=1, tiled=True)  18.1 us
    add x15, other arithmetic, join_partials(): summed = first[2] * left[..., None] + second[2] * right[..., None]  16.1 us
    all_gather x1, blocking collectives, body(): lax.all_gather(partial_proj, 'head')  13.9 us
    all_gather x1, waiting for transfers between devices, merged(): gathered = jax.tree.map(lambda a: lax.all_gather(a, axis), part)  13.5 us
  transfers between devices with their start and end apart: 1, of which 1 were waited for; matrix products, arithmetic and copies ran while one was open for 1% of the time, Pallas kernels for 0%

profile of v1, /device:TPU:1, one launch (start us, length us, event | category | flops | bytes accessed | tf_op | source)
XLA Modules:
  0.0 258.6 jit_solution(7811709030089921073)
XLA Ops:
  7.2 0.0 copy-start
  7.2 0.0 all-gather.7.cloned.1.call-start
  7.2 0.9 copy.20
  8.2 0.8 broadcast_compare_fusion
  8.9 0.0 copy-done
  8.9 1.1 fusion.16
  10.1 28.7 %select_reduce_fusion = (f32[8,16]{1,0:T(8,128)S(1)}, f32[8,16,8192]{2,1,0:T(8,128)}) fusion(pred[8,8192]{1,0:T(8,128)(4,1)S(1)} %broadcast_compare_fusion, bf16[8,8192,576]{1,2,0:T(8,128)(2,1)} %param.16, bf16[8,16,576]{2,0,1:T(8,128)(2,1)S(1)} %pad_maximum_fusion), kind=kOutput, calls=%fused_computation.13 | convolution fusion | flops 1211105152 | bytes 79905280 | tf_op jit(solution)/shard_map/bhc,btc->bht/dot_general | solution.py:35
  38.8 27.1 %fusion.3 = f32[8,16,512]{2,1,0:T(8,128)} fusion(bf16[8,8192,576]{1,2,0:T(8,128)(2,1)} %param.16, f32[8,16,8192]{2,1,0:T(8,128)} %get-tuple-element.200, f32[8,16]{1,0:T(8,128)S(1)} %get-tuple-element.199, pred[8,8192]{1,0:T(8,128)(4,1)S(1)} %broadcast_compare_fusion), kind=kOutput, calls=%fused_computation.8 | convolution fusion | flops 1076887552 | bytes 71631360 | tf_op jit(solution)/shard_map/bht,btl->bhl/dot_general | solution.py:40
  65.9 0.0 copy-start.2
  65.9 0.0 copy-start.3
  65.9 0.0 all-gather.7.cloned.1.call-update
  66.0 19.7 %all-gather = f32[128,16]{1,0:T(8,128)S(1)} all-gather(f32[8,16]{1,0:T(8,128)S(1)} %get-tuple-element.199), channel_id=2, replica_groups=mesh['ctx'=16,'head'=8] {'ctx'}, dimensions={0}, use_global_device_ids=true | all-gather | bytes 8704 | tf_op jit(solution)/shard_map/all_gather | solution.py:12
  85.7 3.3 %fusion.11 = f32[8,16]{1,0:T(8,128)S(1)} fusion(f32[8,16,8192]{2,1,0:T(8,128)} %get-tuple-element.200, f32[8,16]{1,0:T(8,128)S(1)} %get-tuple-element.199, pred[8,8192]{1,0:T(8,128)(4,1)S(1)} %broadcast_compare_fusion), kind=kLoop, calls=%fused_computation.20 | loop fusion | flops 3145600 | bytes 4260864 | tf_op jit(solution)/shard_map/reduce_sum | solution.py:39
  89.0 18.5 %all-gather.1 = f32[128,16]{1,0:T(8,128)S(1)} all-gather(f32[8,16]{1,0:T(8,128)S(1)} %fusion.11), channel_id=3, replica_groups=mesh['ctx'=16,'head'=8] {'ctx'}, dimensions={0}, use_global_device_ids=true | all-gather | bytes 8704 | tf_op jit(solution)/shard_map/all_gather | solution.py:12
  107.5 0.0 copy-done.2
  107.5 0.0 copy-done.3
  107.5 0.1 select_reduce_fusion.1
  107.6 13.5 %all-gather.7.cloned.1.call-done = f32[128,16,512]{2,1,0:T(8,128)} async-done(((f32[8,16,512]{2,1,0:T(8,128)}), f32[128,16,512]{2,1,0:T(8,128)}) %all-gather.7.cloned.1.call-update) | async-done | bytes 4194320 | tf_op jit(solution)/shard_map/all_gather | solution.py:12
  121.2 1.0 slice.12
  122.1 16.8 %while.19 = (s32[]{:T(128)}, f32[8,16]{1,0:T(8,128)S(1)}, f32[8,16]{1,0:T(8,128)S(1)}, f32[8,16,512]{2,1,0:T(8,128)S(1)}, f32[16,8,16]{2,1,0:T(8,128)S(1)}, /*in...) while((s32[]{:T(128)}, f32[8,16]{1,0:T(8,128)S(1)}, ...), condition=%wide.region_3.4_spmd, body=%wide.region_2.3_spmd.sunk | while | flops 197381 | bytes 791703 | solution.py:17
  122.2 1.1 fusion.47
  123.3 1.1 fusion.47
  124.4 1.1 fusion.47
  125.5 1.1 fusion.47
  126.7 1.1 fusion.47
  127.8 1.1 fusion.47
  128.9 1.1 fusion.47
  130.0 1.1 fusion.47
  131.1 1.1 fusion.47
  132.3 1.1 fusion.47
  133.4 1.1 fusion.47
  134.5 1.1 fusion.47
  135.6 1.1 fusion.47
  136.7 1.1 fusion.47
  137.9 1.1 fusion.47
  139.0 0.1 divide_convert_fusion
  139.1 3.0 %fusion.26 = f32[8,448]{1,0:T(8,128)S(1)} fusion(bf16[2048,448]{0,1:T(8,128)(2,1)} %param.20, bf16[16,512,128]{2,1,0:T(8,128)(2,1)} %param.19, bf16[8,16,512]{2,1,0:T(8,128)(2,1)S(1)} %divide_convert_fusion), kind=kOutput, calls=%fused_computation.30 | convolution fusion | flops 31473664 | bytes 4077568 | tf_op jit(solution)/shard_map/dot_general | solution.py:80
  142.1 13.9 %all-gather.3 = f32[64,448]{1,0:T(8,128)S(1)} all-gather(f32[8,448]{1,0:T(8,128)S(1)} %fusion.26), channel_id=5, replica_groups=mesh['ctx'=16,'head'=8] {'head'}, dimensions={0}, use_global_device_ids=true | all-gather | bytes 129024 | tf_op jit(solution)/shard_map/all_gather | solution.py:81
  156.0 0.0 copy-start.1
  156.0 18.1 %all-gather.4 = bf16[16,448,8]{1,2,0:T(8,128)(2,1)S(1)} all-gather(bf16[1,448,8]{1,2,0:T(8,128)(2,1)S(1)} %bitcast.61), channel_id=1, replica_groups=mesh['ctx'=16,'head'=8] {'ctx'}, dimensions={0}, use_global_device_ids=true | all-gather | bytes 121856 | tf_op jit(solution)/shard_map/all_gather | solution.py:82
  174.2 0.1 reshape.66
  174.4 0.2 multiply_reduce_fusion
  174.6 2.7 %fusion.8 = f32[8,256]{1,0:T(8,128)S(1)} fusion(bf16[1,7168,256]{2,1,0:T(8,128)(2,1)} %param.21, f32[7168,8]{0,1:T(8,128)S(1)} %reshape.66, f32[8]{0:T(128)S(1)} %add_sqrt_fusion), kind=kOutput, calls=%fused_computation.17 | convolution fusion | flops 29474816 | bytes 3907616 | tf_op jit(solution)/shard_map/dot_general | solution.py:89
  177.2 5.3 %convolution_multiply_fusion.1 = f32[8,7168]{1,0:T(8,128)S(1)} fusion(bf16[1,256,7168]{2,1,0:T(8,128)(2,1)} %param.23, bf16[1,7168,256]{2,1,0:T(8,128)(2,1)} %param.22, f32[8]{0:T(128)S(1)} %select_reduce_fusion.1, f32[8,256]{1,0:T(8,128)S(1)} %fusion.8, f32[7168,8]{0,1:T(8,128)S(1)} %reshape.66, f32[8]{0:T(128)S(1)} %add_sqrt_fusion), kind=kOutput, calls=%fused_computation.11 | convolution fusion | flops 58904576 | bytes 7807040 | tf_op jit(solution)/shard_map/dot_general | solution.py:92
  182.5 0.0 copy-done.1
  182.5 68.6 %all-reduce.2 = bf16[8,7168]{1,0:T(8,128)(2,1)S(1)} all-reduce(f32[8,7168]{1,0:T(8,128)S(1)} %convolution_multiply_fusion.1), channel_id=6, replica_groups=mesh['ctx'=16,'head'=8] {'ctx','head'}, use_global_device_ids=true, to_apply=%region_7.8.clone | all-reduce | flops 57344 | bytes 344064
  251.1 0.7 dynamic-slice_convert_fusion
  (22 shorter events, 0.4 us)
Async XLA Ops:
  7.2 1.8 copy-start
  7.2 114.0 %all-gather.7.cloned.1.call-start = ((), (), s32[]{:S(2)}) async-start(), calls=%async_computation | async-start | bytes 4456448 | tf_op jit(solution)/shard_map/all_gather | solution.py:12
  65.9 41.6 %copy-start.2 = (f32[8,8]{1,0:T(8,128)S(1)}, f32[8,8]{1,0:T(8,128)}, u32[]{:S(2)}) copy-start(f32[8,8]{1,0:T(8,128)} %param.25) | copy-start | bytes 772
  65.9 41.6 %copy-start.3 = (s32[8,8]{1,0:T(8,128)S(1)}, s32[8,8]{1,0:T(8,128)}, u32[]{:S(2)}) copy-start(s32[8,8]{1,0:T(8,128)} %param.24) | copy-start | bytes 772
  156.0 26.5 %copy-start.1 = (bf16[8,448]{1,0:T(8,128)(2,1)}, bf16[8,448]{1,0:T(8,128)(2,1)S(1)}, u32[]{:S(2)}) copy-start(bf16[8,448]{1,0:T(8,128)(2,1)S(1)} %bitcast_reduce_fusion) | copy-start | bytes 21508
Sparse Core Ops, SparseCore 0:
  66.1 55.0 all-gather.6
